TPU v7x, 512 devices: a whole 4x4x16 slice. The times are simulated.
512 devices in a mesh: dp: 32 (over z, core), crow: 4 (over x), ccol: 4 (over y).
Axes of the slice: x: 4, y: 4, z: 16, core: 2. Of those that a mesh axis runs over, the one named last changes fastest.
Arguments:
- data: float32 [16, 262144], P(None, ('dp', 'crow')), may hold values from 0 to 1
- centres: float32 [16, 3072], P(None, 'ccol'), may hold values from 0 to 1
- scales: float32 [16], replicated, may hold values from 0.5 to 1.2
- factor: float32 [3072, 3072], P('crow', 'ccol'), may hold values from -1 to 1, as said below
- block_inv: float32 [12, 256, 256], P('crow'), may hold values from -1 to 2
- iterate: float32 [8, 3072], replicated, may hold values from -6 to 6
- residual: float32 [8, 3072], replicated, may hold values from -6 to 6
- direction: float32 [8, 3072], replicated, may hold values from -6 to 6
Outputs:
- new_iterate: float32 [8, 3072], replicated
- new_residual: float32 [8, 3072], replicated
- new_direction: float32 [8, 3072], replicated
Inputs may be any that keep to these rules, and one draw needn't show every extreme that they name: `factor`: blocks of 256 x 256 on and above the block diagonal are zero.
All inputs are finite; a program needn't handle non-finite values.
Results may differ from a plain program's by a relative error of at most 0.0001.
Values sent between devices are 32-bit elements; how exact they have to be, the bound alone decides.
A program may use at most 64 MiB of HBM per device.

v0:
```python
import jax
import jax.numpy as jnp
from jax import lax
from jax.sharding import PartitionSpec as P

RBLK = 1024
ridge_weight = 0.2
highest = lax.Precision.HIGHEST


def kernel_tile(sample, centre_set, scales):
    scaled_sample = sample / scales[:, None]
    scaled_centres = centre_set / scales[:, None]
    cross_terms = lax.dot_general(
        scaled_centres,
        scaled_sample,
        (((0,), (0,)), ((), ())),
        precision=highest,
        preferred_element_type=jnp.float32,
    )
    distance = (
        jnp.sum(scaled_centres * scaled_centres, axis=0)[:, None]
        + jnp.sum(scaled_sample * scaled_sample, axis=0)[None, :]
        - 2.0 * cross_terms
    )
    return jnp.exp(-0.5 * distance)


def project(weights, tile):
    return jnp.dot(weights, tile, precision=highest, preferred_element_type=jnp.float32)


def pullback(images, tile):
    return lax.dot_general(
        images,
        tile,
        (((1,), (1,)), ((), ())),
        precision=highest,
        preferred_element_type=jnp.float32,
    )


def per_device(data, centres, scales, factor, block_inv, iterate, residual, direction):
    order = block_inv.shape[1]
    local_rows = factor.shape[0]
    local_cols = factor.shape[1]
    per_row = local_rows // order
    per_col = local_cols // order
    nblocks = per_row * lax.axis_size("crow")
    row_place = lax.axis_index("crow")
    col_place = lax.axis_index("ccol")
    solved = jnp.zeros_like(direction)
    for number in reversed(range(nblocks)):
        start = number * order
        owner = number // per_col
        offset = number % per_col * order
        held = number % per_row
        segment = lax.dynamic_slice_in_dim(solved, row_place * local_rows, local_rows, 1)
        partial_value = project(segment, factor[:, offset : offset + order])
        partial_value = jnp.where(col_place == owner, partial_value, 0.0)
        partial_value = lax.psum(partial_value, ("crow", "ccol"))
        piece = project(direction[:, start : start + order] - partial_value, block_inv[held])
        solved = solved.at[:, start : start + order].set(piece)
    own_part = lax.dynamic_slice_in_dim(solved, row_place * local_rows, local_rows, 1)
    solved = lax.all_gather(own_part, "crow", axis=1, tiled=True)
    rows_here = data.shape[1]
    span = min(RBLK, rows_here)
    blocks = rows_here // span
    stacked = data.reshape(data.shape[0], blocks, span).transpose(1, 0, 2)
    width = centres.shape[1]
    mine = lax.dynamic_slice_in_dim(solved, col_place * width, width, 1)

    def forward_images(carry, sample):
        return (carry, project(mine, kernel_tile(sample, centres, scales)))

    _, images = lax.scan(forward_images, jnp.zeros((), jnp.float32), stacked)
    images = lax.psum(images, "ccol")

    def backward_images(total, pair):
        sample, image_rows = pair
        return (total + pullback(image_rows, kernel_tile(sample, centres, scales)), None)

    summed, _ = lax.scan(
        backward_images, jnp.zeros((solved.shape[0], width), jnp.float32), (stacked, images)
    )
    summed = lax.psum(summed, ("dp", "crow"))
    summed = lax.all_gather(summed, "ccol", axis=1, tiled=True)
    total_rows = rows_here * lax.axis_size("dp") * lax.axis_size("crow")
    normal_image = summed / total_rows + ridge_weight * solved
    image = jnp.zeros_like(direction)
    for number in range(nblocks):
        start = number * order
        owner = number // per_row
        held = number % per_row
        offset = held * order
        segment = lax.dynamic_slice_in_dim(image, col_place * local_cols, local_cols, 1)
        leading = jnp.where(col_place == 0, normal_image[:, start : start + order], 0.0)
        term = pullback(
            leading - pullback(segment, factor[offset : offset + order, :]), block_inv[held]
        )
        term = jnp.where(row_place == owner, term, 0.0)
        piece = lax.psum(term, ("crow", "ccol"))
        image = image.at[:, start : start + order].set(piece)
    gamma = jnp.sum(residual * residual, axis=1)
    curvature = jnp.sum(direction * image, axis=1)
    alpha = (gamma / curvature)[:, None]
    new_iterate = iterate + alpha * direction
    new_residual = residual - alpha * image
    gamma_next = jnp.sum(new_residual * new_residual, axis=1)
    new_direction = new_residual + (gamma_next / gamma)[:, None] * direction
    return (new_iterate, new_residual, new_direction)


def solution(mesh):
    placed = (
        P(None, ("dp", "crow")),
        P(None, "ccol"),
        P(),
        P("crow", "ccol"),
        P("crow", None, None),
        P(),
        P(),
        P(),
    )
    return jax.shard_map(
        per_device, mesh=mesh, in_specs=placed, out_specs=(P(), P(), P()), check_vma=False
    )
```

profile of v0, /device:TPU:8, one launch (start us, length us, event | category | flops | bytes accessed | tf_op | source)
XLA Modules:
  0.0 1564.1 jit_solution(2935731484131593567)
XLA Ops:
  14.5 1.5 convolution_select_fusion.34
  16.1 41.8 %psum.182 = f32[8,256]{1,0:T(8,128)S(1)} all-reduce(f32[8,256]{1,0:T(8,128)S(1)} %convolution_select_fusion.34), channel_id=1, replica_groups=mesh['dp'=32,'crow'=4,'ccol'=4] {'crow','ccol'}, use_global_device_ids=true, to_apply=%region_2.3 | all-reduce | flops 2048 | bytes 16384 | tf_op jit(solution)/shard_map/psum | solution.py:61
  57.9 1.2 fusion.98
  59.0 1.6 convolution_select_fusion.33
  60.6 36.0 %psum.183 = f32[8,256]{1,0:T(8,128)S(1)} all-reduce(f32[8,256]{1,0:T(8,128)S(1)} %convolution_select_fusion.33), channel_id=1, replica_groups=mesh['dp'=32,'crow'=4,'ccol'=4] {'crow','ccol'}, use_global_device_ids=true, to_apply=%region_4.5 | all-reduce | flops 2048 | bytes 16384 | tf_op jit(solution)/shard_map/psum | solution.py:61
  96.6 1.8 fusion.50
  98.9 38.1 %psum.184 = f32[8,256]{1,0:T(8,128)S(1)} all-reduce(f32[8,256]{1,0:T(8,128)S(1)} %convolution_select_fusion.31), channel_id=1, replica_groups=mesh['dp'=32,'crow'=4,'ccol'=4] {'crow','ccol'}, use_global_device_ids=true, to_apply=%region_6.7 | all-reduce | flops 2048 | bytes 16384 | tf_op jit(solution)/shard_map/psum | solution.py:61
  137.0 1.4 fusion.49
  138.8 35.9 %psum.185 = f32[8,256]{1,0:T(8,128)S(1)} all-reduce(f32[8,256]{1,0:T(8,128)S(1)} %convolution_select_fusion.29), channel_id=1, replica_groups=mesh['dp'=32,'crow'=4,'ccol'=4] {'crow','ccol'}, use_global_device_ids=true, to_apply=%region_8.9 | all-reduce | flops 2048 | bytes 16384 | tf_op jit(solution)/shard_map/psum | solution.py:61
  176.1 38.2 %psum.186 = f32[8,256]{1,0:T(8,128)S(1)} all-reduce(f32[8,256]{1,0:T(8,128)S(1)} %convolution_select_fusion.27), channel_id=1, replica_groups=mesh['dp'=32,'crow'=4,'ccol'=4] {'crow','ccol'}, use_global_device_ids=true, to_apply=%region_10.11 | all-reduce | flops 2048 | bytes 16384 | tf_op jit(solution)/shard_map/psum | solution.py:61
  214.2 0.9 fusion.47
  215.6 36.0 %psum.187 = f32[8,256]{1,0:T(8,128)S(1)} all-reduce(f32[8,256]{1,0:T(8,128)S(1)} %convolution_select_fusion.25), channel_id=1, replica_groups=mesh['dp'=32,'crow'=4,'ccol'=4] {'crow','ccol'}, use_global_device_ids=true, to_apply=%region_12.13 | all-reduce | flops 2048 | bytes 16384 | tf_op jit(solution)/shard_map/psum | solution.py:61
  252.7 38.0 %psum.188 = f32[8,256]{1,0:T(8,128)S(1)} all-reduce(f32[8,256]{1,0:T(8,128)S(1)} %convolution_select_fusion.23), channel_id=1, replica_groups=mesh['dp'=32,'crow'=4,'ccol'=4] {'crow','ccol'}, use_global_device_ids=true, to_apply=%region_14.15 | all-reduce | flops 2048 | bytes 16384 | tf_op jit(solution)/shard_map/psum | solution.py:61
  291.9 36.0 %psum.189 = f32[8,256]{1,0:T(8,128)S(1)} all-reduce(f32[8,256]{1,0:T(8,128)S(1)} %convolution_select_fusion.21), channel_id=1, replica_groups=mesh['dp'=32,'crow'=4,'ccol'=4] {'crow','ccol'}, use_global_device_ids=true, to_apply=%region_16.17 | all-reduce | flops 2048 | bytes 16384 | tf_op jit(solution)/shard_map/psum | solution.py:61
  329.2 38.0 %psum.190 = f32[8,256]{1,0:T(8,128)S(1)} all-reduce(f32[8,256]{1,0:T(8,128)S(1)} %convolution_select_fusion.19), channel_id=1, replica_groups=mesh['dp'=32,'crow'=4,'ccol'=4] {'crow','ccol'}, use_global_device_ids=true, to_apply=%region_18.19 | all-reduce | flops 2048 | bytes 16384 | tf_op jit(solution)/shard_map/psum | solution.py:61
  368.4 36.0 %psum.191 = f32[8,256]{1,0:T(8,128)S(1)} all-reduce(f32[8,256]{1,0:T(8,128)S(1)} %convolution_select_fusion.17), channel_id=1, replica_groups=mesh['dp'=32,'crow'=4,'ccol'=4] {'crow','ccol'}, use_global_device_ids=true, to_apply=%region_20.21 | all-reduce | flops 2048 | bytes 16384 | tf_op jit(solution)/shard_map/psum | solution.py:61
  405.6 38.0 %psum.192 = f32[8,256]{1,0:T(8,128)S(1)} all-reduce(f32[8,256]{1,0:T(8,128)S(1)} %convolution_select_fusion.15), channel_id=1, replica_groups=mesh['dp'=32,'crow'=4,'ccol'=4] {'crow','ccol'}, use_global_device_ids=true, to_apply=%region_22.23 | all-reduce | flops 2048 | bytes 16384 | tf_op jit(solution)/shard_map/psum | solution.py:61
  444.9 36.0 %psum.193 = f32[8,256]{1,0:T(8,128)S(1)} all-reduce(f32[8,256]{1,0:T(8,128)S(1)} %convolution_select_fusion.13), channel_id=1, replica_groups=mesh['dp'=32,'crow'=4,'ccol'=4] {'crow','ccol'}, use_global_device_ids=true, to_apply=%region_23.24 | all-reduce | flops 2048 | bytes 16384 | tf_op jit(solution)/shard_map/psum | solution.py:61
  481.7 12.1 all_gather.6
  494.6 0.9 copy.11
  495.6 12.0 while.45
  495.6 2.7 fusion.219
  498.5 3.1 fusion.220
  501.6 2.7 fusion.219
  504.5 3.1 fusion.220
  507.6 1.0 multiply_reduce_fusion.6
  508.7 55.2 %all-reduce.4.cloned.1.call-done = f32[2,8,1024]{2,1,0:T(8,128)} async-done(((f32[2,8,1024]{2,1,0:T(8,128)}), f32[2,8,1024]{2,1,0:T(8,128)}) %all-reduce.4.cloned.1.call-update) | async-done | bytes 65552 | tf_op jit(solution)/shard_map/psum | solution.py:77
  563.9 20.4 %while.46 = (s32[]{:T(128)}, f32[8,768]{1,0:T(8,128)}, f32[2,8,1024]{2,1,0:T(8,128)}, f32[16]{0:T(128)S(1)}, f32[16,768]{1,0:T(8,128)S(1)}, /*index=5*/f32[2,16,1024]{2,1,0:T(8,128)S(1)}, s32[]{:T(128)}, s32[]{:T(128)}) while((s32[]{:T(128)}, f32[8,768]{1,0:T(8,128)}, f32[2,8,1024]{2,1,0:T(8,128)}, f32[16]{0:T(128)S(1)}, ...), condition=%wide.region_32.33_spmd.clone, body=%wide.region_29.32_spmd.clone.sunk | while | flops 229763328 | bytes 6618855 | solution.py:83
  563.9 4.4 fusion.223
  568.5 5.6 fusion.224
  574.1 4.4 fusion.223
  578.6 5.6 fusion.224
  584.3 494.7 %psum.195 = f32[8,768]{1,0:T(8,128)S(1)} all-reduce(f32[8,768]{1,0:T(8,128)} %get-tuple-element.356), channel_id=1, replica_groups=mesh['dp'=32,'crow'=4,'ccol'=4] {'dp','crow'}, use_global_device_ids=true, to_apply=%region_33.34 | all-reduce | flops 6144 | bytes 49152 | tf_op jit(solution)/shard_map/psum | solution.py:86
  1079.0 11.8 all_gather.7
  1091.8 37.8 %psum.196 = f32[8,256]{1,0:T(8,128)S(1)} all-reduce(f32[8,256]{1,0:T(8,128)S(1)} %convolution_select_fusion.11), channel_id=1, replica_groups=mesh['dp'=32,'crow'=4,'ccol'=4] {'crow','ccol'}, use_global_device_ids=true, to_apply=%region_34.35 | all-reduce | flops 2048 | bytes 16384 | tf_op jit(solution)/shard_map/psum | solution.py:102
  1131.2 36.5 %psum.197 = f32[8,256]{1,0:T(8,128)S(1)} all-reduce(f32[8,256]{1,0:T(8,128)S(1)} %convolution_select_fusion.10), channel_id=1, replica_groups=mesh['dp'=32,'crow'=4,'ccol'=4] {'crow','ccol'}, use_global_device_ids=true, to_apply=%region_35.36 | all-reduce | flops 2048 | bytes 16384 | tf_op jit(solution)/shard_map/psum | solution.py:102
  1169.3 37.6 %psum.198 = f32[8,256]{1,0:T(8,128)S(1)} all-reduce(f32[8,256]{1,0:T(8,128)S(1)} %convolution_select_fusion.9), channel_id=1, replica_groups=mesh['dp'=32,'crow'=4,'ccol'=4] {'crow','ccol'}, use_global_device_ids=true, to_apply=%region_36.37 | all-reduce | flops 2048 | bytes 16384 | tf_op jit(solution)/shard_map/psum | solution.py:102
  1208.4 36.6 %psum.199 = f32[8,256]{1,0:T(8,128)S(1)} all-reduce(f32[8,256]{1,0:T(8,128)S(1)} %convolution_select_fusion.8), channel_id=1, replica_groups=mesh['dp'=32,'crow'=4,'ccol'=4] {'crow','ccol'}, use_global_device_ids=true, to_apply=%region_37.38 | all-reduce | flops 2048 | bytes 16384 | tf_op jit(solution)/shard_map/psum | solution.py:102
  1246.7 37.5 %psum.200 = f32[8,256]{1,0:T(8,128)S(1)} all-reduce(f32[8,256]{1,0:T(8,128)S(1)} %convolution_select_fusion.7), channel_id=1, replica_groups=mesh['dp'=32,'crow'=4,'ccol'=4] {'crow','ccol'}, use_global_device_ids=true, to_apply=%region_38.39 | all-reduce | flops 2048 | bytes 16384 | tf_op jit(solution)/shard_map/psum | solution.py:102
  1285.8 36.5 %psum.201 = f32[8,256]{1,0:T(8,128)S(1)} all-reduce(f32[8,256]{1,0:T(8,128)S(1)} %convolution_select_fusion.6), channel_id=1, replica_groups=mesh['dp'=32,'crow'=4,'ccol'=4] {'crow','ccol'}, use_global_device_ids=true, to_apply=%region_39.40 | all-reduce | flops 2048 | bytes 16384 | tf_op jit(solution)/shard_map/psum | solution.py:102
  1324.0 37.5 %psum.202 = f32[8,256]{1,0:T(8,128)S(1)} all-reduce(f32[8,256]{1,0:T(8,128)S(1)} %convolution_select_fusion.5), channel_id=1, replica_groups=mesh['dp'=32,'crow'=4,'ccol'=4] {'crow','ccol'}, use_global_device_ids=true, to_apply=%region_40.41 | all-reduce | flops 2048 | bytes 16384 | tf_op jit(solution)/shard_map/psum | solution.py:102
  1363.1 36.5 %psum.203 = f32[8,256]{1,0:T(8,128)S(1)} all-reduce(f32[8,256]{1,0:T(8,128)S(1)} %convolution_select_fusion.4), channel_id=1, replica_groups=mesh['dp'=32,'crow'=4,'ccol'=4] {'crow','ccol'}, use_global_device_ids=true, to_apply=%region_41.42 | all-reduce | flops 2048 | bytes 16384 | tf_op jit(solution)/shard_map/psum | solution.py:102
  1401.3 37.6 %psum.204 = f32[8,256]{1,0:T(8,128)S(1)} all-reduce(f32[8,256]{1,0:T(8,128)S(1)} %convolution_select_fusion.3), channel_id=1, replica_groups=mesh['dp'=32,'crow'=4,'ccol'=4] {'crow','ccol'}, use_global_device_ids=true, to_apply=%region_42.43 | all-reduce | flops 2048 | bytes 16384 | tf_op jit(solution)/shard_map/psum | solution.py:102
  1440.5 36.5 %psum.205 = f32[8,256]{1,0:T(8,128)S(1)} all-reduce(f32[8,256]{1,0:T(8,128)S(1)} %convolution_select_fusion.2), channel_id=1, replica_groups=mesh['dp'=32,'crow'=4,'ccol'=4] {'crow','ccol'}, use_global_device_ids=true, to_apply=%region_43.44 | all-reduce | flops 2048 | bytes 16384 | tf_op jit(solution)/shard_map/psum | solution.py:102
  1478.6 37.5 %psum.206 = f32[8,256]{1,0:T(8,128)S(1)} all-reduce(f32[8,256]{1,0:T(8,128)S(1)} %convolution_select_fusion.1), channel_id=1, replica_groups=mesh['dp'=32,'crow'=4,'ccol'=4] {'crow','ccol'}, use_global_device_ids=true, to_apply=%region_44.45 | all-reduce | flops 2048 | bytes 16384 | tf_op jit(solution)/shard_map/psum | solution.py:102
  1517.8 36.5 %psum.207 = f32[8,256]{1,0:T(8,128)S(1)} all-reduce(f32[8,256]{1,0:T(8,128)S(1)} %convolution_select_fusion), channel_id=1, replica_groups=mesh['dp'=32,'crow'=4,'ccol'=4] {'crow','ccol'}, use_global_device_ids=true, to_apply=%region_45.46 | all-reduce | flops 2048 | bytes 16384 | tf_op jit(solution)/shard_map/psum | solution.py:102
  1554.4 1.1 multiply_reduce_fusion.4
  1555.5 1.7 multiply_add_fusion
  (100 shorter events, 38.6 us)
Async XLA Ops:
  7.2 91.3 %copy-start = (f32[768,768]{1,0:T(8,128)S(1)}, f32[768,768]{1,0:T(8,128)}, u32[]{:S(2)}) copy-start(f32[768,768]{1,0:T(8,128)} %param.63) | copy-start | bytes 7077892
  7.2 129.8 %copy-start.1 = (f32[3,256,256]{2,1,0:T(8,128)S(1)}, f32[3,256,256]{2,1,0:T(8,128)}, u32[]{:S(2)}) copy-start(f32[3,256,256]{2,1,0:T(8,128)} %param.64) | copy-start | bytes 2359300
  7.2 167.6 %copy-start.3 = (f32[8,3072]{1,0:T(8,128)S(1)}, f32[8,3072]{1,0:T(8,128)}, u32[]{:S(2)}) copy-start(f32[8,3072]{1,0:T(8,128)} %param.67) | copy-start | bytes 294916
  7.2 556.7 %all-reduce.4.cloned.1.call-start = ((), (), s32[]{:S(2)}) async-start(), calls=%async_computation | async-start | bytes 131072 | tf_op jit(solution)/shard_map/psum | solution.py:77
  328.7 165.1 %copy-start.6 = (f32[16,2048]{1,0:T(8,128)S(1)}, f32[16,2048]{1,0:T(8,128)}, u32[]{:S(2)}) copy-start(f32[16,2048]{1,0:T(8,128)} %param.60) | copy-start | bytes 393220
  329.2 166.4 %copy-start.2 = (f32[16,768]{1,0:T(8,128)S(1)}, f32[16,768]{1,0:T(8,128)}, u32[]{:S(2)}) copy-start(f32[16,768]{1,0:T(8,128)} %param.61) | copy-start | bytes 147460
  329.2 166.4 %copy-start.4 = (f32[16]{0:T(128)S(1)}, f32[16]{0:T(128)}, u32[]{:S(2)}) copy-start(f32[16]{0:T(128)} %param.62) | copy-start | bytes 196
  1555.5 1.7 copy-start.5
Sparse Core Ops, SparseCore 0:
  507.7 56.0 all-reduce.3
where the time goes:
time: 1570 us; the launch traced here: 1560 us
  blocking collectives  1410 us (90%)
  matrix products  62.8 us (4%)
  waiting for transfers between devices  55.2 us (4%)
  other arithmetic  18.8 us (1%)
    psum x1, blocking collectives, per_device(): summed = lax.psum(summed, ('dp', 'crow'))  495 us
    psum x12, blocking collectives, per_device(): partial_value = lax.psum(partial_value, ('crow', 'ccol'))  448 us
    psum x12, blocking collectives, per_device(): piece = lax.psum(term, ('crow', 'ccol'))  445 us
    psum x1, waiting for transfers between devices, per_device(): images = lax.psum(images, 'ccol')  55.2 us
  transfers between devices with their start and end apart: 1, of which 1 were waited for; matrix products, arithmetic and copies ran while one was open for 0% of the time, Pallas kernels for 0%

commit v1 on v0

--- a/solution.py
+++ b/solution.py
@@ -83,7 +83,7 @@
     summed, _ = lax.scan(
         backward_images, jnp.zeros((solved.shape[0], width), jnp.float32), (stacked, images)
     )
-    summed = lax.psum(summed, ("dp", "crow"))
+    summed = lax.psum(lax.psum(summed, "dp"), "crow")
     summed = lax.all_gather(summed, "ccol", axis=1, tiled=True)
     total_rows = rows_here * lax.axis_size("dp") * lax.axis_size("crow")
     normal_image = summed / total_rows + ridge_weight * solved

time: 1570 us -> 1180 us (0.75)
  blocking collectives: 1410 us -> 1030 us
    psum x1 -> x2, blocking collectives: 495 us -> 109 us  [per_device(): summed = lax.psum(lax.psum(summed, 'dp'), 'crow')]
where the time goes in v1:
time: 1180 us
  blocking collectives  1030 us (87%)
  matrix products  62.8 us (5%)
  waiting for transfers between devices  55.2 us (5%)
  other arithmetic  18.8 us (2%)
  between operations  14.5 us (1%)
    psum x12, blocking collectives, per_device(): partial_value = lax.psum(partial_value, ('crow', 'ccol'))  448 us
    psum x12, blocking collectives, per_device(): piece = lax.psum(term, ('crow', 'ccol'))  445 us
    psum x2, blocking collectives, per_device(): summed = lax.psum(lax.psum(summed, 'dp'), 'crow')  109 us
    psum x1, waiting for transfers between devices, per_device(): images = lax.psum(images, 'ccol')  55.2 us
    dot_general x26, matrix products, project(): jnp.dot(weights, tile, precision=highest, preferred_element_type=jnp.floa...  25.4 us
  transfers between devices with their start and end apart: 1, of which 1 were waited for; matrix products, arithmetic and copies ran while one was open for 0% of the time, Pallas kernels for 0%

profile of v1, /device:TPU:8, one launch (start us, length us, event | category | flops | bytes accessed | tf_op | source)
XLA Modules:
  0.0 1178.5 jit_solution(17888177584574075347)
XLA Ops:
  14.5 1.5 convolution_select_fusion.34
  16.1 41.8 %psum.189 = f32[8,256]{1,0:T(8,128)S(1)} all-reduce(f32[8,256]{1,0:T(8,128)S(1)} %convolution_select_fusion.34), channel_id=1, replica_groups=mesh['dp'=32,'crow'=4,'ccol'=4] {'crow','ccol'}, use_global_device_ids=true, to_apply=%region_2.3 | all-reduce | flops 2048 | bytes 16384 | tf_op jit(solution)/shard_map/psum | solution.py:61
  57.9 1.2 fusion.98
  59.0 1.6 convolution_select_fusion.33
  60.6 36.0 %psum.190 = f32[8,256]{1,0:T(8,128)S(1)} all-reduce(f32[8,256]{1,0:T(8,128)S(1)} %convolution_select_fusion.33), channel_id=1, replica_groups=mesh['dp'=32,'crow'=4,'ccol'=4] {'crow','ccol'}, use_global_device_ids=true, to_apply=%region_4.5 | all-reduce | flops 2048 | bytes 16384 | tf_op jit(solution)/shard_map/psum | solution.py:61
  96.6 1.8 fusion.50
  98.9 38.1 %psum.191 = f32[8,256]{1,0:T(8,128)S(1)} all-reduce(f32[8,256]{1,0:T(8,128)S(1)} %convolution_select_fusion.31), channel_id=1, replica_groups=mesh['dp'=32,'crow'=4,'ccol'=4] {'crow','ccol'}, use_global_device_ids=true, to_apply=%region_6.7 | all-reduce | flops 2048 | bytes 16384 | tf_op jit(solution)/shard_map/psum | solution.py:61
  137.0 1.4 fusion.49
  138.8 35.9 %psum.192 = f32[8,256]{1,0:T(8,128)S(1)} all-reduce(f32[8,256]{1,0:T(8,128)S(1)} %convolution_select_fusion.29), channel_id=1, replica_groups=mesh['dp'=32,'crow'=4,'ccol'=4] {'crow','ccol'}, use_global_device_ids=true, to_apply=%region_8.9 | all-reduce | flops 2048 | bytes 16384 | tf_op jit(solution)/shard_map/psum | solution.py:61
  176.1 38.2 %psum.193 = f32[8,256]{1,0:T(8,128)S(1)} all-reduce(f32[8,256]{1,0:T(8,128)S(1)} %convolution_select_fusion.27), channel_id=1, replica_groups=mesh['dp'=32,'crow'=4,'ccol'=4] {'crow','ccol'}, use_global_device_ids=true, to_apply=%region_10.11 | all-reduce | flops 2048 | bytes 16384 | tf_op jit(solution)/shard_map/psum | solution.py:61
  215.6 36.0 %psum.194 = f32[8,256]{1,0:T(8,128)S(1)} all-reduce(f32[8,256]{1,0:T(8,128)S(1)} %convolution_select_fusion.25), channel_id=1, replica_groups=mesh['dp'=32,'crow'=4,'ccol'=4] {'crow','ccol'}, use_global_device_ids=true, to_apply=%region_12.13 | all-reduce | flops 2048 | bytes 16384 | tf_op jit(solution)/shard_map/psum | solution.py:61
  252.7 38.0 %psum.195 = f32[8,256]{1,0:T(8,128)S(1)} all-reduce(f32[8,256]{1,0:T(8,128)S(1)} %convolution_select_fusion.23), channel_id=1, replica_groups=mesh['dp'=32,'crow'=4,'ccol'=4] {'crow','ccol'}, use_global_device_ids=true, to_apply=%region_14.15 | all-reduce | flops 2048 | bytes 16384 | tf_op jit(solution)/shard_map/psum | solution.py:61
  291.9 36.0 %psum.196 = f32[8,256]{1,0:T(8,128)S(1)} all-reduce(f32[8,256]{1,0:T(8,128)S(1)} %convolution_select_fusion.21), channel_id=1, replica_groups=mesh['dp'=32,'crow'=4,'ccol'=4] {'crow','ccol'}, use_global_device_ids=true, to_apply=%region_16.17 | all-reduce | flops 2048 | bytes 16384 | tf_op jit(solution)/shard_map/psum | solution.py:61
  329.2 38.0 %psum.197 = f32[8,256]{1,0:T(8,128)S(1)} all-reduce(f32[8,256]{1,0:T(8,128)S(1)} %convolution_select_fusion.19), channel_id=1, replica_groups=mesh['dp'=32,'crow'=4,'ccol'=4] {'crow','ccol'}, use_global_device_ids=true, to_apply=%region_18.19 | all-reduce | flops 2048 | bytes 16384 | tf_op jit(solution)/shard_map/psum | solution.py:61
  368.4 36.0 %psum.198 = f32[8,256]{1,0:T(8,128)S(1)} all-reduce(f32[8,256]{1,0:T(8,128)S(1)} %convolution_select_fusion.17), channel_id=1, replica_groups=mesh['dp'=32,'crow'=4,'ccol'=4] {'crow','ccol'}, use_global_device_ids=true, to_apply=%region_20.21 | all-reduce | flops 2048 | bytes 16384 | tf_op jit(solution)/shard_map/psum | solution.py:61
  405.6 38.0 %psum.199 = f32[8,256]{1,0:T(8,128)S(1)} all-reduce(f32[8,256]{1,0:T(8,128)S(1)} %convolution_select_fusion.15), channel_id=1, replica_groups=mesh['dp'=32,'crow'=4,'ccol'=4] {'crow','ccol'}, use_global_device_ids=true, to_apply=%region_22.23 | all-reduce | flops 2048 | bytes 16384 | tf_op jit(solution)/shard_map/psum | solution.py:61
  444.9 36.0 %psum.200 = f32[8,256]{1,0:T(8,128)S(1)} all-reduce(f32[8,256]{1,0:T(8,128)S(1)} %convolution_select_fusion.13), channel_id=1, replica_groups=mesh['dp'=32,'crow'=4,'ccol'=4] {'crow','ccol'}, use_global_device_ids=true, to_apply=%region_23.24 | all-reduce | flops 2048 | bytes 16384 | tf_op jit(solution)/shard_map/psum | solution.py:61
  481.7 12.1 %all_gather.6 = f32[8,3072]{1,0:T(8,128)S(1)} all-gather(f32[8,768]{1,0:T(8,128)S(1)} %constant_dynamic-slice_fusion.1), channel_id=1, replica_groups=mesh['dp'=32,'crow'=4,'ccol'=4] {'crow'}, dimensions={1}, use_global_device_ids=true | all-gather | bytes 122880 | tf_op jit(solution)/shard_map/all_gather | solution.py:65
  494.6 0.9 copy.11
  495.6 12.0 %while.45 = (s32[]{:T(128)}, f32[2,8,1024]{2,1,0:T(8,128)}, f32[16]{0:T(128)S(1)}, f32[16,768]{1,0:T(8,128)S(1)}, f32[2,16,1024]{2,1,0:T(8,128)S(1)}, /*index=5*/f32[8,768]{1,0:T(8,128)S(1)}, s32[]{:T(128)}) while((s32[]{:T(128)}, f32[2,8,1024]{2,1,0:T(8,128)}, f32[16]{0:T(128)S(1)}, f32[16,768]{1,0:T(8,128)S(1)}, ...), condition=%wide.region_27.28_spmd, body=%wide.region_24.27_spmd.sunk | while | flops 229751040 | bytes 6594261 | solution.py:76
  495.6 2.7 fusion.219
  498.5 3.1 fusion.220
  501.6 2.7 fusion.219
  504.5 3.1 fusion.220
  507.6 1.0 multiply_reduce_fusion.6
  508.7 55.2 %all-reduce.4.cloned.1.call-done = f32[2,8,1024]{2,1,0:T(8,128)} async-done(((f32[2,8,1024]{2,1,0:T(8,128)}), f32[2,8,1024]{2,1,0:T(8,128)}) %all-reduce.4.cloned.1.call-update) | async-done | bytes 65552 | tf_op jit(solution)/shard_map/psum | solution.py:77
  563.9 20.4 %while.46 = (s32[]{:T(128)}, f32[8,768]{1,0:T(8,128)}, f32[2,8,1024]{2,1,0:T(8,128)}, f32[16]{0:T(128)S(1)}, f32[16,768]{1,0:T(8,128)S(1)}, /*index=5*/f32[2,16,1024]{2,1,0:T(8,128)S(1)}, s32[]{:T(128)}, s32[]{:T(128)}) while((s32[]{:T(128)}, f32[8,768]{1,0:T(8,128)}, f32[2,8,1024]{2,1,0:T(8,128)}, f32[16]{0:T(128)S(1)}, ...), condition=%wide.region_32.33_spmd.clone, body=%wide.region_29.32_spmd.clone.sunk | while | flops 229763328 | bytes 6618855 | solution.py:83
  563.9 4.4 fusion.223
  568.5 5.6 fusion.224
  574.1 4.4 fusion.223
  578.6 5.6 fusion.224
  584.3 91.7 %psum.202 = f32[8,768]{1,0:T(8,128)S(1)} all-reduce(f32[8,768]{1,0:T(8,128)} %get-tuple-element.356), channel_id=1, replica_groups=mesh['dp'=32,'crow'=4,'ccol'=4] {'dp'}, use_global_device_ids=true, to_apply=%region_33.34 | all-reduce | flops 6144 | bytes 49152 | tf_op jit(solution)/shard_map/psum | solution.py:86
  675.9 17.0 %psum.203 = f32[8,768]{1,0:T(8,128)S(1)} all-reduce(f32[8,768]{1,0:T(8,128)S(1)} %psum.202), channel_id=1, replica_groups=mesh['dp'=32,'crow'=4,'ccol'=4] {'crow'}, use_global_device_ids=true, to_apply=%region_34.35 | all-reduce | flops 6144 | bytes 49152 | tf_op jit(solution)/shard_map/psum | solution.py:86
  692.9 11.8 %all_gather.7 = f32[8,3072]{1,0:T(8,128)S(1)} all-gather(f32[8,768]{1,0:T(8,128)S(1)} %psum.203), channel_id=1, replica_groups=mesh['dp'=32,'crow'=4,'ccol'=4] {'ccol'}, dimensions={1}, use_global_device_ids=true | all-gather | bytes 122880 | tf_op jit(solution)/shard_map/all_gather | solution.py:87
  705.7 37.8 %psum.204 = f32[8,256]{1,0:T(8,128)S(1)} all-reduce(f32[8,256]{1,0:T(8,128)S(1)} %convolution_select_fusion.11), channel_id=1, replica_groups=mesh['dp'=32,'crow'=4,'ccol'=4] {'crow','ccol'}, use_global_device_ids=true, to_apply=%region_35.36 | all-reduce | flops 2048 | bytes 16384 | tf_op jit(solution)/shard_map/psum | solution.py:102
  745.2 37.0 %psum.205 = f32[8,256]{1,0:T(8,128)S(1)} all-reduce(f32[8,256]{1,0:T(8,128)S(1)} %convolution_select_fusion.10), channel_id=1, replica_groups=mesh['dp'=32,'crow'=4,'ccol'=4] {'crow','ccol'}, use_global_device_ids=true, to_apply=%region_36.37 | all-reduce | flops 2048 | bytes 16384 | tf_op jit(solution)/shard_map/psum | solution.py:102
  783.8 37.1 %psum.206 = f32[8,256]{1,0:T(8,128)S(1)} all-reduce(f32[8,256]{1,0:T(8,128)S(1)} %convolution_select_fusion.9), channel_id=1, replica_groups=mesh['dp'=32,'crow'=4,'ccol'=4] {'crow','ccol'}, use_global_device_ids=true, to_apply=%region_37.38 | all-reduce | flops 2048 | bytes 16384 | tf_op jit(solution)/shard_map/psum | solution.py:102
  822.4 37.0 %psum.207 = f32[8,256]{1,0:T(8,128)S(1)} all-reduce(f32[8,256]{1,0:T(8,128)S(1)} %convolution_select_fusion.8), channel_id=1, replica_groups=mesh['dp'=32,'crow'=4,'ccol'=4] {'crow','ccol'}, use_global_device_ids=true, to_apply=%region_38.39 | all-reduce | flops 2048 | bytes 16384 | tf_op jit(solution)/shard_map/psum | solution.py:102
  861.1 37.0 %psum.208 = f32[8,256]{1,0:T(8,128)S(1)} all-reduce(f32[8,256]{1,0:T(8,128)S(1)} %convolution_select_fusion.7), channel_id=1, replica_groups=mesh['dp'=32,'crow'=4,'ccol'=4] {'crow','ccol'}, use_global_device_ids=true, to_apply=%region_39.40 | all-reduce | flops 2048 | bytes 16384 | tf_op jit(solution)/shard_map/psum | solution.py:102
  899.8 37.0 %psum.209 = f32[8,256]{1,0:T(8,128)S(1)} all-reduce(f32[8,256]{1,0:T(8,128)S(1)} %convolution_select_fusion.6), channel_id=1, replica_groups=mesh['dp'=32,'crow'=4,'ccol'=4] {'crow','ccol'}, use_global_device_ids=true, to_apply=%region_40.41 | all-reduce | flops 2048 | bytes 16384 | tf_op jit(solution)/shard_map/psum | solution.py:102
  938.4 37.0 %psum.210 = f32[8,256]{1,0:T(8,128)S(1)} all-reduce(f32[8,256]{1,0:T(8,128)S(1)} %convolution_select_fusion.5), channel_id=1, replica_groups=mesh['dp'=32,'crow'=4,'ccol'=4] {'crow','ccol'}, use_global_device_ids=true, to_apply=%region_41.42 | all-reduce | flops 2048 | bytes 16384 | tf_op jit(solution)/shard_map/psum | solution.py:102
  977.0 37.0 %psum.211 = f32[8,256]{1,0:T(8,128)S(1)} all-reduce(f32[8,256]{1,0:T(8,128)S(1)} %convolution_select_fusion.4), channel_id=1, replica_groups=mesh['dp'=32,'crow'=4,'ccol'=4] {'crow','ccol'}, use_global_device_ids=true, to_apply=%region_42.43 | all-reduce | flops 2048 | bytes 16384 | tf_op jit(solution)/shard_map/psum | solution.py:102
  1015.7 37.1 %psum.212 = f32[8,256]{1,0:T(8,128)S(1)} all-reduce(f32[8,256]{1,0:T(8,128)S(1)} %convolution_select_fusion.3), channel_id=1, replica_groups=mesh['dp'=32,'crow'=4,'ccol'=4] {'crow','ccol'}, use_global_device_ids=true, to_apply=%region_43.44 | all-reduce | flops 2048 | bytes 16384 | tf_op jit(solution)/shard_map/psum | solution.py:102
  1054.4 37.0 %psum.213 = f32[8,256]{1,0:T(8,128)S(1)} all-reduce(f32[8,256]{1,0:T(8,128)S(1)} %convolution_select_fusion.2), channel_id=1, replica_groups=mesh['dp'=32,'crow'=4,'ccol'=4] {'crow','ccol'}, use_global_device_ids=true, to_apply=%region_44.45 | all-reduce | flops 2048 | bytes 16384 | tf_op jit(solution)/shard_map/psum | solution.py:102
  1093.0 37.1 %psum.214 = f32[8,256]{1,0:T(8,128)S(1)} all-reduce(f32[8,256]{1,0:T(8,128)S(1)} %convolution_select_fusion.1), channel_id=1, replica_groups=mesh['dp'=32,'crow'=4,'ccol'=4] {'crow','ccol'}, use_global_device_ids=true, to_apply=%region_45.46 | all-reduce | flops 2048 | bytes 16384 | tf_op jit(solution)/shard_map/psum | solution.py:102
  1131.7 37.0 %psum.215 = f32[8,256]{1,0:T(8,128)S(1)} all-reduce(f32[8,256]{1,0:T(8,128)S(1)} %convolution_select_fusion), channel_id=1, replica_groups=mesh['dp'=32,'crow'=4,'ccol'=4] {'crow','ccol'}, use_global_device_ids=true, to_apply=%region_46.47 | all-reduce | flops 2048 | bytes 16384 | tf_op jit(solution)/shard_map/psum | solution.py:102
  1168.8 1.1 multiply_reduce_fusion.4
  1169.9 1.7 multiply_add_fusion
  (101 shorter events, 39.5 us)
Async XLA Ops:
  7.2 91.3 %copy-start = (f32[768,768]{1,0:T(8,128)S(1)}, f32[768,768]{1,0:T(8,128)}, u32[]{:S(2)}) copy-start(f32[768,768]{1,0:T(8,128)} %param.63) | copy-start | bytes 7077892
  7.2 129.8 %copy-start.1 = (f32[3,256,256]{2,1,0:T(8,128)S(1)}, f32[3,256,256]{2,1,0:T(8,128)}, u32[]{:S(2)}) copy-start(f32[3,256,256]{2,1,0:T(8,128)} %param.64) | copy-start | bytes 2359300
  7.2 167.6 %copy-start.3 = (f32[8,3072]{1,0:T(8,128)S(1)}, f32[8,3072]{1,0:T(8,128)}, u32[]{:S(2)}) copy-start(f32[8,3072]{1,0:T(8,128)} %param.67) | copy-start | bytes 294916
  7.2 556.7 %all-reduce.4.cloned.1.call-start = ((), (), s32[]{:S(2)}) async-start(), calls=%async_computation | async-start | bytes 131072 | tf_op jit(solution)/shard_map/psum | solution.py:77
  328.7 165.1 %copy-start.6 = (f32[16,2048]{1,0:T(8,128)S(1)}, f32[16,2048]{1,0:T(8,128)}, u32[]{:S(2)}) copy-start(f32[16,2048]{1,0:T(8,128)} %param.60) | copy-start | bytes 393220
  329.2 166.4 %copy-start.2 = (f32[16,768]{1,0:T(8,128)S(1)}, f32[16,768]{1,0:T(8,128)}, u32[]{:S(2)}) copy-start(f32[16,768]{1,0:T(8,128)} %param.61) | copy-start | bytes 147460
  329.2 166.4 %copy-start.4 = (f32[16]{0:T(128)S(1)}, f32[16]{0:T(128)}, u32[]{:S(2)}) copy-start(f32[16]{0:T(128)} %param.62) | copy-start | bytes 196
  1169.9 1.7 copy-start.5
Sparse Core Ops, SparseCore 0:
  507.7 56.0 all-reduce.3
